TPU v7x, 32 devices: a whole 2x2x4 slice. The times are simulated.
32 devices in a mesh: wave: 32 (over z, y, x, core), lev: 1.
Axes of the slice: x: 2, y: 2, z: 4, core: 2. Of those that a mesh axis runs over, the one named last changes fastest.
Arguments:
- fourier: bfloat16 [2560, 16, 4, 128], P('wave', 'lev'), may hold values from -6 to 6
- owner: int32 [64], replicated, may hold values from 0 to 63, each once
- legendre: bfloat16 [64, 2, 640, 1280], P('wave'), may hold values from -0.125 to 0.125
- quad_weights: float32 [1280], replicated, may hold values from 0.5 to 2
- layer_depth: float32 [16], P('lev'), may hold values from 0.05 to 0.3
Outputs:
- fields_out: bfloat16 [2560, 16, 4, 128], P('wave', 'lev')
- geopotential: bfloat16 [2560, 16, 128], P('wave', 'lev')
Inputs may be any that keep to these rules, and one draw needn't show every extreme that they name: owner is a permutation of the slots; slot s lies on index s // 2 of wave.
All inputs are finite; a program needn't handle non-finite values.
Results may differ from a plain program's by a relative error of at most 0.0063.
Values may be sent and summed in bfloat16 or wider, within the bound.
A program may use at most 64 MiB of HBM per device.

v0:
```python
import jax
import jax.numpy as jnp
from jax import lax
from jax.sharding import PartitionSpec as P

BLOCK = 128


def prefix(part, axis, combine, identity):
    count = lax.axis_size(axis)
    place = lax.axis_index(axis)
    ahead = count - 1 - place
    gathered = lax.all_gather(part, axis)
    state = jnp.zeros_like(part) + jnp.asarray(identity, part.dtype)

    def one(turn, state):
        source = count - 1 - turn
        return combine(state, lax.dynamic_index_in_dim(gathered, source, 0, False))

    return lax.fori_loop(0, ahead, one, state)


def fold_halves(columns, quad_weights):
    values = columns.astype(jnp.float32)
    half_lats = quad_weights.shape[0]
    northern = values[:half_lats]
    southern = values[half_lats:][::-1]
    scaled = quad_weights[:, None]
    return (
        (scaled * (northern + southern)).astype(jnp.bfloat16),
        (scaled * (northern - southern)).astype(jnp.bfloat16),
    )


def legendre_pair(tables, folded, length):
    column_count = folded[0].shape[1]
    halves = []
    for parity in range(2):
        live_rows = (length - parity + 1) // 2
        block_count = (live_rows + BLOCK - 1) // BLOCK
        source = folded[parity]
        parity_table = tables[parity]

        def add_block(
            block_index, totals, parity_table=parity_table, source=source, live_rows=live_rows
        ):
            start = block_index * BLOCK
            rows_here = lax.dynamic_slice_in_dim(parity_table, start, BLOCK, 0)
            spectra = jnp.dot(rows_here, source, preferred_element_type=jnp.float32)
            positions = start + jnp.arange(BLOCK, dtype=jnp.int32)
            spectra = jnp.where((positions < live_rows)[:, None], spectra, 0.0).astype(jnp.bfloat16)
            return totals + lax.dot_general(
                rows_here, spectra, (((0,), (0,)), ((), ())), preferred_element_type=jnp.float32
            )

        zeros_start = jnp.zeros((tables.shape[2], column_count), jnp.float32)
        halves.append(lax.fori_loop(0, block_count, add_block, zeros_start))
    upper = halves[0] + halves[1]
    lower = halves[0] - halves[1]
    return jnp.concatenate([upper, lower[::-1]], axis=0).astype(jnp.bfloat16)


def on_device(fourier, owner, legendre, quad_weights, layer_depth):
    lat_rows, level_count, field_count, doubled = fourier.shape
    waves = doubled // 2
    slots = legendre.shape[0]
    degrees = 2 * legendre.shape[2]
    slot_ids = jnp.arange(waves, dtype=jnp.int32)
    matches = owner[None, :] == slot_ids[:, None]
    wave_of_slot = jnp.sum(jnp.where(matches, slot_ids[None, :], 0), axis=1)
    my_waves = lax.dynamic_slice_in_dim(wave_of_slot, lax.axis_index("wave") * slots, slots, 0)
    lengths = degrees - my_waves * degrees // waves
    unpacked = fourier.reshape(lat_rows, level_count, field_count, 2, waves)
    ordered = jnp.take(unpacked, wave_of_slot, axis=4)
    outgoing = jnp.transpose(ordered, (4, 0, 1, 2, 3)).reshape(
        waves, lat_rows, level_count * field_count * 2
    )
    arrived = lax.all_to_all(outgoing, "wave", split_axis=0, concat_axis=1, tiled=True)
    results = [
        legendre_pair(
            legendre[slot_index],
            fold_halves(arrived[slot_index], quad_weights),
            lengths[slot_index],
        )
        for slot_index in range(slots)
    ]
    stacked = jnp.stack(results, axis=0)
    returned = lax.all_to_all(stacked, "wave", split_axis=1, concat_axis=0, tiled=True)
    restored = jnp.take(returned, owner, axis=0).reshape(
        waves, lat_rows, level_count, field_count, 2
    )
    fields_out = jnp.transpose(restored, (1, 2, 3, 4, 0)).reshape(
        lat_rows, level_count, field_count, doubled
    )
    contrib = layer_depth[None, :, None] * fields_out[:, :, 0, :].astype(jnp.float32)
    inside = jnp.cumsum(contrib[:, ::-1], axis=1)[:, ::-1]
    layer_total = inside[:, 0]
    below = prefix(layer_total, "lev", jnp.add, jnp.zeros_like(layer_total))
    geopotential = (below[:, None, :] + inside - 0.5 * contrib).astype(jnp.bfloat16)
    return (fields_out, geopotential)


def solution(mesh):
    return jax.shard_map(
        on_device,
        mesh=mesh,
        in_specs=(P("wave", "lev", None, None), P(), P("wave", None, None, None), P(), P("lev")),
        out_specs=(P("wave", "lev", None, None), P("wave", "lev", None)),
        check_vma=False,
    )
```

profile of v0, /device:TPU:0, one launch (start us, length us, event | category | flops | bytes accessed | tf_op | source)
XLA Modules:
  0.0 154.8 jit_solution(15132614563999653883)
XLA Ops:
  0.6 0.8 select_reduce_fusion
  1.4 3.1 %copy.55 = bf16[80,16,4,128]{0,3,2,1:T(8,128)(2,1)S(1)} copy(bf16[80,16,4,128]{3,2,1,0:T(4,128)(2,1)} %param.13) | data formatting | bytes 2621440 | tf_op args[0]
  4.5 2.7 %copy.56 = bf16[80,16,4,2,64]{0,1,3,2,4:T(8,128)(2,1)} copy(bf16[80,16,4,2,64]{0,4,3,2,1:T(8,128)(2,1)S(1)} %bitcast.83) | data formatting | bytes 2621440 | tf_op jit(solution)/shard_map/reshape | solution.py:73
  7.2 2.5 %gather_fusion = bf16[64,80,16,4,2]{1,2,4,3,0:T(8,128)(2,1)S(1)} fusion(bf16[80,16,4,2,64]{0,1,3,2,4:T(8,128)(2,1)} %copy.56, s32[1024]{0:T(1024)S(1)} %pad_clamp_fusion.1), kind=kCustom, calls=%fused_computation | custom fusion | bytes 2621696 | tf_op jit(solution)/shard_map/jit(_take)/gather | solution.py:74
  10.0 1.4 copy.57
  11.4 2.7 %copy.58 = bf16[64,80,128]{2,1,0:T(8,128)(2,1)} copy(bf16[64,80,128]{1,0,2:T(8,128)(2,1)S(1)} %bitcast.82) | data formatting | bytes 2621440 | tf_op jit(solution)/shard_map/reshape | solution.py:75
  14.1 7.3 %all-to-all-start = ((bf16[64,80,128]{2,1,0:T(8,128)(2,1)}), bf16[64,80,128]{2,1,0:T(8,128)(2,1)S(1)}, u32[]{:S(2)}, u32[]{:S(2)}) async-start(bf16[64,80,128]{2,1,0:T(8,128)(2,1)} %copy.58), calls=%async_computation | async-start | bytes 2621440 | tf_op jit(solution)/shard_map/all_to_all | solution.py:78
  21.5 0.6 fusion.47
  28.2 5.2 %slice_bitcast_fusion.2 = (bf16[640,1280]{1,0:T(8,128)(2,1)}, bf16[640,1280]{1,0:T(8,128)(2,1)}, bf16[640,1280]{1,0:T(8,128)(2,1)}, bf16[640,1280]{1,0:T(8,128)(2,1)S(1)}) fusion(bf16[2,2,640,1280]{3,2,1,0:T(8,128)(2,1)} %param.15), kind=kLoop, calls=%fused_computation.43 | loop fusion | bytes 13107200 | tf_op jit(solution)/shard_map/squeeze | solution.py:42
  33.5 20.1 %all-to-all-done = bf16[64,80,128]{2,1,0:T(8,128)(2,1)S(1)} async-done(((bf16[64,80,128]{2,1,0:T(8,128)(2,1)}), bf16[64,80,128]{2,1,0:T(8,128)(2,1)S(1)}, u32[]{:S(2)}, u32[]{:S(2)}) %all-to-all-start) | async-done | bytes 1310752 | tf_op jit(solution)/shard_map/all_to_all | solution.py:78
  53.7 1.3 fusion.45
  55.0 3.3 %rev.18 = f32[1280,128]{1,0:T(8,128)} reverse(f32[1280,128]{1,0:T(8,128)S(1)} %bitcast.88), dimensions={0} | reverse | bytes 1310720 | tf_op jit(solution)/shard_map/rev | solution.py:27
  58.3 3.2 %rev.20 = f32[1280,128]{1,0:T(8,128)} reverse(f32[1280,128]{1,0:T(8,128)S(1)} %bitcast.87), dimensions={0} | reverse | bytes 1310720 | tf_op jit(solution)/shard_map/rev | solution.py:27
  61.5 2.9 %fusion.40 = (bf16[1280,128]{1,0:T(8,128)(2,1)S(1)}, bf16[1280,128]{1,0:T(8,128)(2,1)}, bf16[1280,128]{1,0:T(8,128)(2,1)S(1)}, bf16[1280,128]{1,0:T(8,128)(2,1)}) fusion(f32[1280,128]{1,0:T(8,128)} %rev.18, f32[1,16,80,128]{3,2,0,1:T(8,128)} %get-tuple-element.224, f32[1280]{0:T(1024)S(1)} %copy-done.2, f32[1280,128]{1,0:T(8,128)} %rev.20, ...), kind=kLoop, calls=%fused_computation.60 | loop fusion | flops 1966080 | bytes 3937280 | tf_op jit(solution)/shard_map/convert_element_type | solution.py:31
  64.5 8.1 %while.46 = (s32[]{:T(128)}, f32[1280,128]{1,0:T(8,128)S(1)}, s32[]{:T(128)}, bf16[640,1280]{1,0:T(8,128)(2,1)}, s32[]{:T(128)}, /*index=5*/bf16[1280,128]{1,0:T...) while((s32[]{:T(128)}, f32[1280,128]{1,0:T(8,128)S(1)}, s32[]{:T(128)}, ...), condition=%wide.region_4.5_spmd, body=%wide.region_3.4_spmd.sunk | while | flops 84082952 | bytes 2295195 | solution.py:57
  64.5 1.6 %convolution_add_fusion.9 = f32[1280,128]{1,0:T(8,128)S(1)} fusion(f32[1280,128]{1,0:T(8,128)S(1)} %get-tuple-element.489, bf16[1280,128]{1,0:T(8,128)(2,1)S(1)} %get-tuple-element.503, bf16[640,1280]{1,0:T(8,128)(2,1)} %get-tuple-element.501, s32[]{:T(128)S(6)} %select_n.164, pred[128]{0:T(512)(128)(4,1)S(1)} %add_compare_fusion.9), kind=kOutput, calls=%fused_computation.11.clone.1 | convolution fusion | flops 84082688 | bytes 2294912 | tf_op jit(solution)/shard_map/while/body/dot_general | solution.py:52
  66.1 1.6 %convolution_add_fusion.9 = f32[1280,128]{1,0:T(8,128)S(1)} fusion(f32[1280,128]{1,0:T(8,128)S(1)} %get-tuple-element.489, bf16[1280,128]{1,0:T(8,128)(2,1)S(1)} %get-tuple-element.503, bf16[640,1280]{1,0:T(8,128)(2,1)} %get-tuple-element.501, s32[]{:T(128)S(6)} %select_n.164, pred[128]{0:T(512)(128)(4,1)S(1)} %add_compare_fusion.9), kind=kOutput, calls=%fused_computation.11.clone.1 | convolution fusion | flops 84082688 | bytes 2294912 | tf_op jit(solution)/shard_map/while/body/dot_general | solution.py:52
  67.7 1.6 %convolution_add_fusion.9 = f32[1280,128]{1,0:T(8,128)S(1)} fusion(f32[1280,128]{1,0:T(8,128)S(1)} %get-tuple-element.489, bf16[1280,128]{1,0:T(8,128)(2,1)S(1)} %get-tuple-element.503, bf16[640,1280]{1,0:T(8,128)(2,1)} %get-tuple-element.501, s32[]{:T(128)S(6)} %select_n.164, pred[128]{0:T(512)(128)(4,1)S(1)} %add_compare_fusion.9), kind=kOutput, calls=%fused_computation.11.clone.1 | convolution fusion | flops 84082688 | bytes 2294912 | tf_op jit(solution)/shard_map/while/body/dot_general | solution.py:52
  69.4 1.6 %convolution_add_fusion.9 = f32[1280,128]{1,0:T(8,128)S(1)} fusion(f32[1280,128]{1,0:T(8,128)S(1)} %get-tuple-element.489, bf16[1280,128]{1,0:T(8,128)(2,1)S(1)} %get-tuple-element.503, bf16[640,1280]{1,0:T(8,128)(2,1)} %get-tuple-element.501, s32[]{:T(128)S(6)} %select_n.164, pred[128]{0:T(512)(128)(4,1)S(1)} %add_compare_fusion.9), kind=kOutput, calls=%fused_computation.11.clone.1 | convolution fusion | flops 84082688 | bytes 2294912 | tf_op jit(solution)/shard_map/while/body/dot_general | solution.py:52
  71.0 1.6 %convolution_add_fusion.9 = f32[1280,128]{1,0:T(8,128)S(1)} fusion(f32[1280,128]{1,0:T(8,128)S(1)} %get-tuple-element.489, bf16[1280,128]{1,0:T(8,128)(2,1)S(1)} %get-tuple-element.503, bf16[640,1280]{1,0:T(8,128)(2,1)} %get-tuple-element.501, s32[]{:T(128)S(6)} %select_n.164, pred[128]{0:T(512)(128)(4,1)S(1)} %add_compare_fusion.9), kind=kOutput, calls=%fused_computation.11.clone.1 | convolution fusion | flops 84082688 | bytes 2294912 | tf_op jit(solution)/shard_map/while/body/dot_general | solution.py:52
  72.6 8.6 %while.45 = (s32[]{:T(128)}, f32[1280,128]{1,0:T(8,128)S(1)}, s32[]{:T(128)}, bf16[640,1280]{1,0:T(8,128)(2,1)}, s32[]{:T(128)}, /*index=5*/bf16[1280,128]{1,0:T...) while((s32[]{:T(128)}, f32[1280,128]{1,0:T(8,128)S(1)}, s32[]{:T(128)}, bf16[640,1280]{1,0:T(8,128)(2,1)}, ...), condition=%wide.region_2.3_spmd, body=%wide.region_1.2_spmd.sunk | while | flops 84082952 | bytes 2295195 | solution.py:57
  72.7 1.7 %convolution_add_fusion.8 = f32[1280,128]{1,0:T(8,128)S(1)} fusion(f32[1280,128]{1,0:T(8,128)S(1)} %get-tuple-element.459, bf16[1280,128]{1,0:T(8,128)(2,1)} %get-tuple-element.473, bf16[640,1280]{1,0:T(8,128)(2,1)} %get-tuple-element.471, s32[]{:T(128)S(6)} %select_n.162, pred[128]{0:T(512)(128)(4,1)S(1)} %add_compare_fusion.8), kind=kOutput, calls=%fused_computation.2.clone.1 | convolution fusion | flops 84082688 | bytes 2294912 | tf_op jit(solution)/shard_map/while/body/dot_general | solution.py:52
  74.4 1.7 %convolution_add_fusion.8 = f32[1280,128]{1,0:T(8,128)S(1)} fusion(f32[1280,128]{1,0:T(8,128)S(1)} %get-tuple-element.459, bf16[1280,128]{1,0:T(8,128)(2,1)} %get-tuple-element.473, bf16[640,1280]{1,0:T(8,128)(2,1)} %get-tuple-element.471, s32[]{:T(128)S(6)} %select_n.162, pred[128]{0:T(512)(128)(4,1)S(1)} %add_compare_fusion.8), kind=kOutput, calls=%fused_computation.2.clone.1 | convolution fusion | flops 84082688 | bytes 2294912 | tf_op jit(solution)/shard_map/while/body/dot_general | solution.py:52
  76.1 1.7 %convolution_add_fusion.8 = f32[1280,128]{1,0:T(8,128)S(1)} fusion(f32[1280,128]{1,0:T(8,128)S(1)} %get-tuple-element.459, bf16[1280,128]{1,0:T(8,128)(2,1)} %get-tuple-element.473, bf16[640,1280]{1,0:T(8,128)(2,1)} %get-tuple-element.471, s32[]{:T(128)S(6)} %select_n.162, pred[128]{0:T(512)(128)(4,1)S(1)} %add_compare_fusion.8), kind=kOutput, calls=%fused_computation.2.clone.1 | convolution fusion | flops 84082688 | bytes 2294912 | tf_op jit(solution)/shard_map/while/body/dot_general | solution.py:52
  77.8 1.7 %convolution_add_fusion.8 = f32[1280,128]{1,0:T(8,128)S(1)} fusion(f32[1280,128]{1,0:T(8,128)S(1)} %get-tuple-element.459, bf16[1280,128]{1,0:T(8,128)(2,1)} %get-tuple-element.473, bf16[640,1280]{1,0:T(8,128)(2,1)} %get-tuple-element.471, s32[]{:T(128)S(6)} %select_n.162, pred[128]{0:T(512)(128)(4,1)S(1)} %add_compare_fusion.8), kind=kOutput, calls=%fused_computation.2.clone.1 | convolution fusion | flops 84082688 | bytes 2294912 | tf_op jit(solution)/shard_map/while/body/dot_general | solution.py:52
  79.6 1.7 %convolution_add_fusion.8 = f32[1280,128]{1,0:T(8,128)S(1)} fusion(f32[1280,128]{1,0:T(8,128)S(1)} %get-tuple-element.459, bf16[1280,128]{1,0:T(8,128)(2,1)} %get-tuple-element.473, bf16[640,1280]{1,0:T(8,128)(2,1)} %get-tuple-element.471, s32[]{:T(128)S(6)} %select_n.162, pred[128]{0:T(512)(128)(4,1)S(1)} %add_compare_fusion.8), kind=kOutput, calls=%fused_computation.2.clone.1 | convolution fusion | flops 84082688 | bytes 2294912 | tf_op jit(solution)/shard_map/while/body/dot_general | solution.py:52
  81.3 0.8 fusion.41
  82.0 0.8 sub.72
  82.9 8.6 %while.48 = (s32[]{:T(128)}, f32[1280,128]{1,0:T(8,128)S(1)}, s32[]{:T(128)}, bf16[640,1280]{1,0:T(8,128)(2,1)}, s32[]{:T(128)}, /*index=5*/bf16[1280,128]{1,0:T...) while((s32[]{:T(128)}, f32[1280,128]{1,0:T(8,128)S(1)}, s32[]{:T(128)}, bf16[640,1280]{1,0:T(8,128)(2,1)}, ...), condition=%wide.region_8.9_spmd, body=%wide.region_7.8_spmd.sunk | while | flops 84082952 | bytes 2295195 | solution.py:57
  82.9 1.7 %convolution_add_fusion.11 = f32[1280,128]{1,0:T(8,128)S(1)} fusion(f32[1280,128]{1,0:T(8,128)S(1)} %get-tuple-element.429, bf16[1280,128]{1,0:T(8,128)(2,1)} %get-tuple-element.443, bf16[640,1280]{1,0:T(8,128)(2,1)} %get-tuple-element.441, s32[]{:T(128)S(6)} %select_n.168, pred[128]{0:T(512)(128)(4,1)S(1)} %add_compare_fusion.11), kind=kOutput, calls=%fused_computation.29.clone.1 | convolution fusion | flops 84082688 | bytes 2294912 | tf_op jit(solution)/shard_map/while/body/dot_general | solution.py:52
  84.6 1.7 %convolution_add_fusion.11 = f32[1280,128]{1,0:T(8,128)S(1)} fusion(f32[1280,128]{1,0:T(8,128)S(1)} %get-tuple-element.429, bf16[1280,128]{1,0:T(8,128)(2,1)} %get-tuple-element.443, bf16[640,1280]{1,0:T(8,128)(2,1)} %get-tuple-element.441, s32[]{:T(128)S(6)} %select_n.168, pred[128]{0:T(512)(128)(4,1)S(1)} %add_compare_fusion.11), kind=kOutput, calls=%fused_computation.29.clone.1 | convolution fusion | flops 84082688 | bytes 2294912 | tf_op jit(solution)/shard_map/while/body/dot_general | solution.py:52
  86.4 1.7 %convolution_add_fusion.11 = f32[1280,128]{1,0:T(8,128)S(1)} fusion(f32[1280,128]{1,0:T(8,128)S(1)} %get-tuple-element.429, bf16[1280,128]{1,0:T(8,128)(2,1)} %get-tuple-element.443, bf16[640,1280]{1,0:T(8,128)(2,1)} %get-tuple-element.441, s32[]{:T(128)S(6)} %select_n.168, pred[128]{0:T(512)(128)(4,1)S(1)} %add_compare_fusion.11), kind=kOutput, calls=%fused_computation.29.clone.1 | convolution fusion | flops 84082688 | bytes 2294912 | tf_op jit(solution)/shard_map/while/body/dot_general | solution.py:52
  88.1 1.7 %convolution_add_fusion.11 = f32[1280,128]{1,0:T(8,128)S(1)} fusion(f32[1280,128]{1,0:T(8,128)S(1)} %get-tuple-element.429, bf16[1280,128]{1,0:T(8,128)(2,1)} %get-tuple-element.443, bf16[640,1280]{1,0:T(8,128)(2,1)} %get-tuple-element.441, s32[]{:T(128)S(6)} %select_n.168, pred[128]{0:T(512)(128)(4,1)S(1)} %add_compare_fusion.11), kind=kOutput, calls=%fused_computation.29.clone.1 | convolution fusion | flops 84082688 | bytes 2294912 | tf_op jit(solution)/shard_map/while/body/dot_general | solution.py:52
  89.8 1.7 %convolution_add_fusion.11 = f32[1280,128]{1,0:T(8,128)S(1)} fusion(f32[1280,128]{1,0:T(8,128)S(1)} %get-tuple-element.429, bf16[1280,128]{1,0:T(8,128)(2,1)} %get-tuple-element.443, bf16[640,1280]{1,0:T(8,128)(2,1)} %get-tuple-element.441, s32[]{:T(128)S(6)} %select_n.168, pred[128]{0:T(512)(128)(4,1)S(1)} %add_compare_fusion.11), kind=kOutput, calls=%fused_computation.29.clone.1 | convolution fusion | flops 84082688 | bytes 2294912 | tf_op jit(solution)/shard_map/while/body/dot_general | solution.py:52
  91.6 2.9 %while.47 = (s32[]{:T(128)}, f32[1280,128]{1,0:T(8,128)S(1)}, s32[]{:T(128)}, bf16[640,1280]{1,0:T(8,128)(2,1)S(1)}, s32[]{:T(128)}, /*index=5*/bf16[1280,128]{1...) while((s32[]{:T(128)}, f32[1280,128]{1,0:T(8,128)S(1)}, s32[]{:T(128)}, ...), condition=%wide.region_6.7_spmd, body=%wide.region_5.6_spmd.sunk | while | flops 84082952 | bytes 2295579 | solution.py:57
  92.2 0.5 convolution_add_fusion.10
  93.3 0.5 convolution_add_fusion.10
  94.7 0.8 copy-done.1
  96.3 11.6 %copy.59 = bf16[2,2560,128]{2,0,1:T(2,128)(2,1)} copy(bf16[2,2560,128]{2,1,0:T(8,128)(2,1)S(1)} %maximum_maximum_fusion) | data formatting | bytes 2621440 | tf_op jit(solution)/shard_map/stack | solution.py:87
  107.9 2.8 %all-to-all-start.1 = ((bf16[2,2560,128]{2,0,1:T(2,128)(2,1)}), bf16[2,2560,128]{2,0,1:T(2,128)(2,1)S(1)}, u32[]{:S(2)}, u32[]{:S(2)}) async-start(bf16[2,2560,128]{2,0,1:T(2,128)(2,1)} %copy.59), calls=%async_computation.1 | async-start | bytes 2621440 | tf_op jit(solution)/shard_map/all_to_all | solution.py:88
  110.7 31.8 %all-to-all-done.1 = bf16[2,2560,128]{2,0,1:T(2,128)(2,1)S(1)} async-done(((bf16[2,2560,128]{2,0,1:T(2,128)(2,1)}), bf16[2,2560,128]{2,0,1:T(2,128)(2,1)S(1)}, u32[]{:S(2)}, u32[]{:S(2)}) %all-to-all-start.1) | async-done | bytes 1310752 | tf_op jit(solution)/shard_map/all_to_all | solution.py:88
  142.8 0.8 gather_fusion.1
  143.6 2.7 %copy.62 = bf16[64,80,128]{1,0,2:T(8,128)(2,1)S(1)} copy(bf16[64,80,128]{2,1,0:T(8,128)(2,1)S(1)} %gather_fusion.1) | data formatting | bytes 2621440 | tf_op jit(solution)/shard_map/jit(_take)/gather | solution.py:89
  146.3 2.0 %fusion.32 = bf16[80,16,4,2,64]{0,1,3,2,4:T(8,128)(2,1)S(1)} fusion(bf16[64,80,16,4,2]{1,0,4,3,2:T(8,128)(2,1)S(1)} %bitcast.81, pred[64]{0:T(512)(128)(4,1)S(1)} %compare_and_fusion.1), kind=kLoop, calls=%fused_computation.39 | loop fusion | flops 655360 | bytes 2621504 | tf_op jit(solution)/shard_map/transpose | solution.py:92
  148.3 1.4 copy.64
  149.7 2.4 %copy.66 = bf16[80,16,4,128]{3,2,1,0:T(4,128)(2,1)} copy(bf16[80,16,4,128]{0,3,2,1:T(8,128)(2,1)S(1)} %bitcast.80) | data formatting | bytes 2621440
  152.5 1.3 fusion.48
  154.0 0.8 copy.67
  (57 shorter events, 4.1 us)
Async XLA Ops:
  14.1 39.4 %all-to-all-start = ((bf16[64,80,128]{2,1,0:T(8,128)(2,1)}), bf16[64,80,128]{2,1,0:T(8,128)(2,1)S(1)}, u32[]{:S(2)}, u32[]{:S(2)}) async-start(bf16[64,80,128]{2,1,0:T(8,128)(2,1)} %copy.58), calls=%async_computation | async-start | bytes 2621440 | tf_op jit(solution)/shard_map/all_to_all | solution.py:78
  55.0 6.5 %copy-start.2 = (f32[1280]{0:T(1024)S(1)}, f32[1280]{0:T(1024)}, u32[]{:S(2)}) copy-start(f32[1280]{0:T(1024)} %param.16) | copy-start | bytes 15364
  94.5 1.0 copy-start.1
  94.6 1.6 %copy-start = (bf16[1,1280,128]{2,1,0:T(8,128)(2,1)S(1)}, bf16[1,1280,128]{2,1,0:T(8,128)(2,1)}, u32[]{:S(2)}) copy-start(bf16[1,1280,128]{2,1,0:T(8,128)(2,1)} %fusion.41) | copy-start | bytes 983044
  107.9 2.8 %copy-start.4 = (s32[64]{0:T(128)S(1)}, s32[64]{0:T(128)}, u32[]{:S(2)}) copy-start(s32[64]{0:T(128)} %param.14) | copy-start | bytes 772
  107.9 34.7 %all-to-all-start.1 = ((bf16[2,2560,128]{2,0,1:T(2,128)(2,1)}), bf16[2,2560,128]{2,0,1:T(2,128)(2,1)S(1)}, u32[]{:S(2)}, u32[]{:S(2)}) async-start(bf16[2,2560,128]{2,0,1:T(2,128)(2,1)} %copy.59), calls=%async_computation.1 | async-start | bytes 2621440 | tf_op jit(solution)/shard_map/all_to_all | solution.py:88
  149.7 2.7 %copy-start.3 = (f32[16]{0:T(128)S(1)}, f32[16]{0:T(128)}, u32[]{:S(2)}) copy-start(f32[16]{0:T(128)} %param.17) | copy-start | bytes 196
where the time goes:
time: 154 us; the launch traced here: 155 us
  waiting for transfers between devices  51.9 us (34%)
  local copies, waits for them, and re-layouts  47.8 us (31%)
  matrix products  27.2 us (18%)
  starting transfers between devices  10.1 us (7%)
  other arithmetic  9.7 us (6%)
  between operations  7.14 us (5%)
    all_to_all x1, waiting for transfers between devices, on_device(): lax.all_to_all(stacked, 'wave', split_axis=1, concat_axis=0, tiled=True)  31.8 us
    dot_general x20, matrix products, add_block(): lax.dot_general(rows_here, spectra, (((0,), (0,)), ((), ())), preferred_e...  27.2 us
    all_to_all x1, waiting for transfers between devices, on_device(): lax.all_to_all(outgoing, 'wave', split_axis=0, concat_axis=1, tiled=True)  20.1 us
    another operation x1, local copies, waits for them, and re-layouts, on_device(): stacked = jnp.stack(results, axis=0)  11.6 us
    unnamed x14, local copies, waits for them, and re-layouts  7.34 us
    all_to_all x1, starting transfers between devices, on_device(): lax.all_to_all(outgoing, 'wave', split_axis=0, concat_axis=1, tiled=True)  7.3 us
    rev x2, local copies, waits for them, and re-layouts, fold_halves(): southern = values[half_lats:][::-1]  6.48 us
    squeeze x1, local copies, waits for them, and re-layouts, legendre_pair(): parity_table = tables[parity]  5.22 us
  transfers between devices with their start and end apart: 2, of which 2 were waited for; matrix products, arithmetic and copies ran while one was open for 4% of the time, Pallas kernels for 0%

commit v1 on v0

v1 whole, which is shorter than its diff:
```python
import functools

import jax
import jax.numpy as jnp
from jax import lax
from jax.experimental import pallas as pl
from jax.experimental.pallas import tpu as pltpu
from jax.sharding import PartitionSpec as P

MESH = pl.DeviceIdType.MESH
GROUP = 16
NT = (((1,), (1,)), ((), ()))
TN = (((0,), (0,)), ((), ()))


def kernel(
    n,
    slots,
    degrees,
    x_ref,
    own_ref,
    depth_ref,
    weight_ref,
    table_hbm,
    out_ref,
    geo_ref,
    tables,
    outgoing,
    arrived,
    weights,
    folded,
    spectra,
    results,
    returned,
    table_sem,
    send_sem,
    recv_sem,
    own_sem,
):
    me = lax.axis_index("wave")
    lats, lf, lanes = x_ref.shape
    waves = n * slots
    half = tables.shape[2]
    north = tables.shape[3]
    whole = n * lats
    levels = geo_ref.shape[1]
    fields = lf // levels

    barrier = pltpu.get_barrier_semaphore()

    def greet(step, carry):
        other = lax.rem(me + step, n)
        pl.semaphore_signal(barrier, inc=1, device_id={"wave": other}, device_id_type=MESH)
        return carry

    lax.fori_loop(1, n, greet, 0)

    def table_copy(slot):
        return pltpu.make_async_copy(table_hbm.at[slot], tables.at[slot], table_sem.at[slot])

    for slot in range(slots):
        table_copy(slot).start()

    south = me >= n // 2
    place = jnp.where(south, n // 2 + (n - 1 - me), me)

    def lat_of(turn):
        return jnp.where(south, lats - 1 - turn, turn)

    rows_i = lax.broadcasted_iota(jnp.int32, (lanes, lanes), 0)
    permute = jnp.where(rows_i == own_ref[...], 1.0, 0.0).astype(jnp.bfloat16)
    low = lax.broadcasted_iota(jnp.int32, (waves, lanes), 1) < lf

    def scatter_group(group, carry):
        parts = []
        for pair in range(GROUP // 2):
            turn = group * GROUP + 2 * pair
            two = jnp.concatenate([x_ref[lat_of(turn)], x_ref[lat_of(turn + 1)]], axis=0)
            mixed = lax.dot_general(permute, two, NT, preferred_element_type=jnp.float32)
            real, imag = mixed[:waves], mixed[waves:]
            parts.append(jnp.where(low, real, pltpu.roll(imag, lf, 1)))
            parts.append(jnp.where(low, pltpu.roll(real, lf, 1), imag))
        block = jnp.swapaxes(jnp.stack(parts, axis=0), 0, 1)
        start = pl.multiple_of(group * GROUP, GROUP)
        outgoing[:, pl.ds(start, GROUP), :] = block.astype(jnp.bfloat16)
        return carry

    lax.fori_loop(0, lats // GROUP, scatter_group, 0)
    pl.semaphore_wait(barrier, n - 1)

    def rows(ref, start, count):
        return ref.at[pl.ds(pl.multiple_of(start, GROUP), count), :]

    def partner(turn):
        return lax.rem(
            me + jnp.where(lax.rem(turn, 2) == 0, n // 2 + turn // 2, (turn + 1) // 2), n
        )

    def send_out(slot):
        target = rows(arrived, slot * whole + place * lats, lats)

        def one(turn, carry):
            other = partner(turn)
            pltpu.make_async_remote_copy(
                src_ref=outgoing.at[other * slots + slot],
                dst_ref=target,
                send_sem=send_sem.at[0, slot],
                recv_sem=recv_sem.at[0, slot],
                device_id={"wave": other},
                device_id_type=MESH,
            ).start()
            return carry

        lax.fori_loop(0, n - 1, one, 0)
        own_out(slot).start()

    def own_out(slot):
        return pltpu.make_async_copy(
            outgoing.at[me * slots + slot],
            rows(arrived, slot * whole + place * lats, lats),
            own_sem.at[0, slot],
        )

    def place_of(other):
        return jnp.where(other >= n // 2, n // 2 + (n - 1 - other), other)

    def send_back(slot):
        def one(turn, carry):
            other = partner(turn)
            pltpu.make_async_remote_copy(
                src_ref=rows(results, slot * whole + place_of(other) * lats, lats),
                dst_ref=returned.at[me * slots + slot],
                send_sem=send_sem.at[1, slot],
                recv_sem=recv_sem.at[1, slot],
                device_id={"wave": other},
                device_id_type=MESH,
            ).start()
            return carry

        lax.fori_loop(0, n - 1, one, 0)
        own_back(slot).start()

    def own_back(slot):
        return pltpu.make_async_copy(
            rows(results, slot * whole + place * lats, lats),
            returned.at[me * slots + slot],
            own_sem.at[1, slot],
        )

    def all_of(ref, sem):
        return pltpu.make_async_copy(ref, ref, sem)

    many = (n - 1) * lats
    for slot in range(slots):
        send_out(slot)

    for group in range(north // lanes):
        row = weight_ref[group : group + 1, :]
        weights[group * lanes : (group + 1) * lanes, :] = jnp.transpose(
            jnp.broadcast_to(row, (lanes, lanes))
        )

    lane = lax.broadcasted_iota(jnp.int32, (1, lanes), 1)
    lengths = degrees - (lane * degrees) // waves
    span = 2 * lanes
    part = lanes

    for slot in range(slots):
        table_copy(slot).wait()
        own_out(slot).wait()
        all_of(rows(arrived, slot * whole, many), recv_sem.at[0, slot]).wait()

        def fold(index, carry, slot=slot):
            start = pl.multiple_of(index * span, span)
            upper = arrived[pl.ds(slot * whole + start, span), :].astype(jnp.float32)
            lower = arrived[pl.ds(slot * whole + north + start, span), :].astype(jnp.float32)
            scale = weights[pl.ds(start, span), :]
            folded[0, pl.ds(start, span), :] = (scale * (upper + lower)).astype(jnp.bfloat16)
            folded[1, pl.ds(start, span), :] = (scale * (upper - lower)).astype(jnp.bfloat16)
            return carry

        lax.fori_loop(0, north // span, fold, 0)
        mine = (own_ref[...] == me * slots + slot) & (lane < waves)
        length = jnp.sum(jnp.where(mine, lengths, 0), axis=1, keepdims=True)

        def direct(index, carry, slot=slot, length=length):
            start = pl.multiple_of(index * part, part)
            degree = 2 * (start + lax.broadcasted_iota(jnp.int32, (part, lanes), 0))
            for parity in range(2):
                value = jnp.dot(
                    tables[slot, parity, pl.ds(start, part), :],
                    folded[parity],
                    preferred_element_type=jnp.float32,
                )
                value = jnp.where(degree + parity < length, value, 0.0)
                spectra[parity, pl.ds(start, part), :] = value.astype(jnp.bfloat16)
            return carry

        lax.fori_loop(0, half // part, direct, 0)

        def inverse(index, carry, slot=slot):
            start = pl.multiple_of(index * span, span)
            even, odd = (
                lax.dot_general(
                    tables[slot, parity, :, pl.ds(start, span)],
                    spectra[parity],
                    TN,
                    preferred_element_type=jnp.float32,
                )
                for parity in range(2)
            )
            results[pl.ds(slot * whole + start, span), :] = (even + odd).astype(jnp.bfloat16)
            results[pl.ds(slot * whole + north + start, span), :] = (even - odd).astype(
                jnp.bfloat16
            )
            return carry

        lax.fori_loop(0, north // span, inverse, 0)
        send_back(slot)

    pair_rows = 2 * levels
    row = lax.broadcasted_iota(jnp.int32, (pair_rows, lanes), 0)
    column = lax.broadcasted_iota(jnp.int32, (pair_rows, lanes), 1)
    level, level2 = row % levels, (column % lf) // fields
    depth = depth_ref[...]
    term = jnp.where(level2 > level, depth, jnp.where(level2 == level, 0.5 * depth, 0.0))
    fits = (row // levels == column // lf) & (column % fields == 0)
    term = jnp.where(fits, term, 0.0)
    high = term.astype(jnp.bfloat16)
    rest = (term - high.astype(jnp.float32)).astype(jnp.bfloat16)
    stacked = jnp.concatenate([high, rest], axis=0)

    for slot in range(slots):
        own_back(slot).wait()
        all_of(returned.at[pl.ds(0, n - 1)], recv_sem.at[1, slot]).wait()

    def gather_group(group, carry):
        start = pl.multiple_of(group * GROUP, GROUP)
        block = returned[:, pl.ds(start, GROUP), :].astype(jnp.float32)
        block = jnp.swapaxes(block, 0, 1)
        for pair in range(GROUP // 2):
            turn = group * GROUP + 2 * pair
            first, second = block[2 * pair], block[2 * pair + 1]
            real = jnp.where(low, first, pltpu.roll(second, lf, 1))
            imag = jnp.where(low, pltpu.roll(first, lf, 1), second)
            mixed = jnp.concatenate([real, imag], axis=0).astype(jnp.bfloat16)
            two = lax.dot_general(mixed, permute, TN, preferred_element_type=jnp.float32).astype(
                jnp.bfloat16
            )
            heights = jnp.dot(stacked, two, preferred_element_type=jnp.float32)
            heights = (heights[:pair_rows] + heights[pair_rows:]).astype(jnp.bfloat16)
            for h in range(2):
                lat = lat_of(turn + h)
                out_ref[lat] = two[h * lf : (h + 1) * lf]
                geo_ref[lat] = heights[h * levels : (h + 1) * levels]
        return carry

    lax.fori_loop(0, lats // GROUP, gather_group, 0)

    for slot in range(slots):
        all_of(outgoing.at[pl.ds(0, n - 1)], send_sem.at[0, slot]).wait()
        all_of(rows(results, slot * whole, many), send_sem.at[1, slot]).wait()


def geopotential_over(fields_out, layer_depth):
    contrib = layer_depth[None, :, None] * fields_out[:, :, 0, :].astype(jnp.float32)
    inside = jnp.cumsum(contrib[:, ::-1], axis=1)[:, ::-1]
    gathered = lax.all_gather(inside[:, 0], "lev")
    behind = jnp.arange(gathered.shape[0]) > lax.axis_index("lev")
    below = jnp.sum(jnp.where(behind[:, None, None], gathered, 0.0), axis=0)
    return (below[:, None, :] + inside - 0.5 * contrib).astype(jnp.bfloat16)


def on_device(fourier, owner, legendre, quad_weights, layer_depth):
    n = lax.axis_size("wave")
    lats, levels, fields, lanes = fourier.shape
    lf = levels * fields
    slots, _, half, north = legendre.shape
    waves = n * slots
    whole = n * lats
    assert lanes == 2 * waves and lanes == 2 * lf and whole == 2 * north
    own = jnp.concatenate([owner, owner + waves]).reshape(1, lanes)
    depth = jnp.tile(jnp.repeat(layer_depth, fields), 2).reshape(1, lanes)
    vmem = pl.BlockSpec(memory_space=pltpu.VMEM)
    fields_out, geopotential = pl.pallas_call(
        functools.partial(kernel, n, slots, 2 * half),
        out_shape=(
            jax.ShapeDtypeStruct((lats, lf, lanes), jnp.bfloat16),
            jax.ShapeDtypeStruct((lats, levels, lanes), jnp.bfloat16),
        ),
        in_specs=[vmem] * 4 + [pl.BlockSpec(memory_space=pl.ANY)],
        out_specs=(vmem, vmem),
        scratch_shapes=[
            pltpu.VMEM(legendre.shape, jnp.bfloat16),
            pltpu.VMEM((waves, lats, lanes), jnp.bfloat16),
            pltpu.VMEM((slots * whole, lanes), jnp.bfloat16),
            pltpu.VMEM((north, lanes), jnp.float32),
            pltpu.VMEM((2, north, lanes), jnp.bfloat16),
            pltpu.VMEM((2, half, lanes), jnp.bfloat16),
            pltpu.VMEM((slots * whole, lanes), jnp.bfloat16),
            pltpu.VMEM((waves, lats, lanes), jnp.bfloat16),
            pltpu.SemaphoreType.DMA((slots,)),
            pltpu.SemaphoreType.DMA((2, slots)),
            pltpu.SemaphoreType.DMA((2, slots)),
            pltpu.SemaphoreType.DMA((2, slots)),
        ],
        compiler_params=pltpu.CompilerParams(
            collective_id=0, has_side_effects=True, vmem_limit_bytes=48 * 2**20
        ),
        cost_estimate=pl.CostEstimate(
            flops=16 * slots * half * north * lanes,
            bytes_accessed=2 * legendre.size + 4 * fourier.size,
            transcendentals=0,
        ),
    )(
        fourier.reshape(lats, lf, lanes),
        own,
        depth,
        quad_weights.reshape(north // lanes, lanes),
        legendre,
    )
    fields_out = fields_out.reshape(lats, levels, fields, lanes)
    if lax.axis_size("lev") > 1:
        geopotential = geopotential_over(fields_out, layer_depth)
    return (fields_out, geopotential)


def solution(mesh):
    return jax.shard_map(
        on_device,
        mesh=mesh,
        in_specs=(P("wave", "lev", None, None), P(), P("wave", None, None, None), P(), P("lev")),
        out_specs=(P("wave", "lev", None, None), P("wave", "lev", None)),
        check_vma=False,
    )
```

time: 154 us -> 74.6 us (0.48)
  Pallas kernels: 0 us -> 67.6 us
  waiting for transfers between devices: 51.9 us -> 0 us
  local copies, waits for them, and re-layouts: 47.8 us -> 4.69 us
  matrix products: 27.2 us -> 0 us
  starting transfers between devices: 10.1 us -> 0 us
  other arithmetic: 9.7 us -> 1.39 us
  between operations: 7.14 us -> 0.65 us
    pallas_call x0 -> x1, Pallas kernels: none -> 67.6 us  [on_device(): pl.pallas_call(functools.partial(kernel, n, slots, 2 * half), out_shape=(...]
    all_to_all x2 -> x0, waiting for transfers between devices: 51.9 us -> none  [the longest x1 31.8 us: on_device(): lax.all_to_all(stacked, 'wave', split_axis=1, concat_axis=0, tiled=True)]
    dot_general x20 -> x0, matrix products: 27.2 us -> none  [add_block(): lax.dot_general(rows_here, spectra, (((0,), (0,)), ((), ())), preferred_e...]
    another operation x5 -> x3, local copies, waits for them, and re-layouts: 11.8 us -> 0.17 us  [on_device(): depth = jnp.tile(jnp.repeat(layer_depth, fields), 2).reshape(1, lanes)]
    all_to_all x2 -> x0, starting transfers between devices: 10.1 us -> none  [the longest x1 7.3 us: on_device(): lax.all_to_all(outgoing, 'wave', split_axis=0, concat_axis=1, tiled=True)]
    rev x5 -> x0, local copies, waits for them, and re-layouts: 7.17 us -> none  [the longest x2 6.48 us: fold_halves(): southern = values[half_lats:][::-1]]
    gather x3 -> x0, local copies, waits for them, and re-layouts: 6 us -> none  [the longest x2 3.46 us: on_device(): jnp.take(returned, owner, axis=0)]
    reshape x2 -> x0, local copies, waits for them, and re-layouts: 5.41 us -> none  [the longest x1 2.73 us: on_device(): jnp.transpose(ordered, (4, 0, 1, 2, 3))]
  transfers between devices with their start and end apart: 2 -> 0, of which waited for: 2 -> 0; matrix products, arithmetic and copies ran while one was open for 4% -> 0% of each run, Pallas kernels for 0% -> 0%
where the time goes in v1:
time: 74.6 us; the launch traced here: 74.4 us
  Pallas kernels  67.6 us (91%)
  local copies, waits for them, and re-layouts  4.69 us (6%)
  other arithmetic  1.39 us (2%)
    pallas_call x1, Pallas kernels, on_device(): pl.pallas_call(functools.partial(kernel, n, slots, 2 * half), out_shape=(...  67.6 us
    unnamed x6, local copies, waits for them, and re-layouts  3.8 us

profile of v1, /device:TPU:0, one launch (start us, length us, event | category | flops | bytes accessed | tf_op | source)
XLA Modules:
  0.0 74.4 jit_solution(3682955429338548998)
XLA Ops:
  0.6 0.7 broadcast_add_fusion
  1.3 0.7 add_bitcast_fusion.own_ref
  2.0 0.7 broadcast_in_dim.3
  2.7 0.1 tile.7
  2.8 0.1 reshape_tile.3.depth_ref
  2.9 0.0 copy-start
  2.9 1.3 %copy-done = bf16[80,16,4,128]{3,2,1,0:T(4,128)(2,1)S(1)} copy-done((bf16[80,16,4,128]{3,2,1,0:T(4,128)(2,1)S(1)}, bf16[80,16,4,128]{3,2,1,0:T(4,128)(2,1)}, u32[]{:S(2)}) %copy-start) | copy-done | bytes 1310744
  4.2 0.0 copy-start.1
  4.2 0.7 copy-done.1
  4.9 67.6 %shard_map.68 = (bf16[80,64,128]{2,1,0:T(8,128)(2,1)S(1)}, bf16[80,16,128]{2,1,0:T(8,128)(2,1)S(1)}) custom-call(bf16[80,64,128]{2,1,0:T(8,128)(2,1)S(1)} %bitcast.6, s32[1,128]{1,0:T(1,128)S(1)} %add_bitcast_fusion.own_ref, f32[1,128]{1,0:T(1,128)S(1)} %reshape_tile.3.depth_ref, f32[10,128]{1,0:T(8,128)S(1)} %bitcast.7, bf16[2,2,640,1280]{3,2,1,0:T(8,128)(2,1)} %table_hbm.1), custom_call_target="tpu_custom_call" | custom-call | flops 3355443200 | bytes 9175040 | tf_op jit(solution)/shard_map/pallas_call | solution.py:285
  72.6 1.1 %copy.9 = bf16[80,16,4,128]{3,2,1,0:T(4,128)(2,1)} copy(bf16[80,16,4,128]{3,2,1,0:T(4,128)(2,1)S(1)} %bitcast.5) | data formatting | bytes 2621440
  73.6 0.7 copy.10
  (1 shorter events, 0.0 us)
Async XLA Ops:
  2.9 1.3 %copy-start = (bf16[80,16,4,128]{3,2,1,0:T(4,128)(2,1)S(1)}, bf16[80,16,4,128]{3,2,1,0:T(4,128)(2,1)}, u32[]{:S(2)}) copy-start(bf16[80,16,4,128]{3,2,1,0:T(4,128)(2,1)} %param.5) | copy-start | bytes 3932164
  4.2 0.7 copy-start.1

commit v2 on v1

--- a/solution.py
+++ b/solution.py
@@ -17,13 +17,17 @@
     n,
     slots,
     degrees,
-    x_ref,
+    x_hbm,
     own_ref,
     depth_ref,
     weight_ref,
     table_hbm,
+    out_hbm,
+    geo_hbm,
+    x_ref,
     out_ref,
     geo_ref,
+    own_row,
     tables,
     outgoing,
     arrived,
@@ -32,6 +36,8 @@
     spectra,
     results,
     returned,
+    x_sem,
+    out_sem,
     table_sem,
     send_sem,
     recv_sem,
@@ -55,23 +61,48 @@
 
     lax.fori_loop(1, n, greet, 0)
 
+    south = me >= n // 2
+    groups = lats // GROUP
+
+    def lats_of(group):
+        return pl.ds(jnp.where(south, lats - GROUP - group * GROUP, group * GROUP), GROUP)
+
+    def out_copies(group):
+        piece = lats_of(group)
+        return (
+            pltpu.make_async_copy(out_ref.at[piece], out_hbm.at[piece], out_sem.at[0, group]),
+            pltpu.make_async_copy(geo_ref.at[piece], geo_hbm.at[piece], out_sem.at[1, group]),
+        )
+
+    def x_copy(group):
+        piece = lats_of(group)
+        return pltpu.make_async_copy(x_hbm.at[piece], x_ref.at[piece], x_sem.at[group])
+
+    for group in range(groups):
+        x_copy(group).start()
+
     def table_copy(slot):
         return pltpu.make_async_copy(table_hbm.at[slot], tables.at[slot], table_sem.at[slot])
 
     for slot in range(slots):
         table_copy(slot).start()
 
-    south = me >= n // 2
     place = jnp.where(south, n // 2 + (n - 1 - me), me)
 
     def lat_of(turn):
         return jnp.where(south, lats - 1 - turn, turn)
 
     rows_i = lax.broadcasted_iota(jnp.int32, (lanes, lanes), 0)
-    permute = jnp.where(rows_i == own_ref[...], 1.0, 0.0).astype(jnp.bfloat16)
+    lane = lax.broadcasted_iota(jnp.int32, (1, lanes), 1)
+    owner = jnp.zeros((1, lanes), jnp.int32)
+    for wave in range(waves):
+        owner = jnp.where(lane % waves == wave, own_ref[wave], owner)
+    own_row[...] = owner + waves * (lane // waves)
+    permute = jnp.where(rows_i == own_row[...], 1.0, 0.0).astype(jnp.bfloat16)
     low = lax.broadcasted_iota(jnp.int32, (waves, lanes), 1) < lf
 
     def scatter_group(group, carry):
+        x_copy(group).wait()
         parts = []
         for pair in range(GROUP // 2):
             turn = group * GROUP + 2 * pair
@@ -85,7 +116,8 @@
         outgoing[:, pl.ds(start, GROUP), :] = block.astype(jnp.bfloat16)
         return carry
 
-    lax.fori_loop(0, lats // GROUP, scatter_group, 0)
+    first = (groups + 1) // 2
+    lax.fori_loop(0, first, scatter_group, 0)
     pl.semaphore_wait(barrier, n - 1)
 
     def rows(ref, start, count):
@@ -96,13 +128,13 @@
             me + jnp.where(lax.rem(turn, 2) == 0, n // 2 + turn // 2, (turn + 1) // 2), n
         )
 
-    def send_out(slot):
-        target = rows(arrived, slot * whole + place * lats, lats)
+    def send_out(slot, begin, count):
+        target = rows(arrived, slot * whole + place * lats + begin, count)
 
         def one(turn, carry):
             other = partner(turn)
             pltpu.make_async_remote_copy(
-                src_ref=outgoing.at[other * slots + slot],
+                src_ref=outgoing.at[other * slots + slot, pl.ds(begin, count)],
                 dst_ref=target,
                 send_sem=send_sem.at[0, slot],
                 recv_sem=recv_sem.at[0, slot],
@@ -112,7 +144,6 @@
             return carry
 
         lax.fori_loop(0, n - 1, one, 0)
-        own_out(slot).start()
 
     def own_out(slot):
         return pltpu.make_async_copy(
@@ -124,21 +155,20 @@
     def place_of(other):
         return jnp.where(other >= n // 2, n // 2 + (n - 1 - other), other)
 
-    def send_back(slot):
+    def send_back(slot, begin, count, sem):
         def one(turn, carry):
             other = partner(turn)
             pltpu.make_async_remote_copy(
-                src_ref=rows(results, slot * whole + place_of(other) * lats, lats),
-                dst_ref=returned.at[me * slots + slot],
+                src_ref=rows(results, slot * whole + place_of(other) * lats + begin, count),
+                dst_ref=returned.at[me * slots + slot, pl.ds(begin, count)],
                 send_sem=send_sem.at[1, slot],
-                recv_sem=recv_sem.at[1, slot],
+                recv_sem=recv_sem.at[1, sem],
                 device_id={"wave": other},
                 device_id_type=MESH,
             ).start()
             return carry
 
         lax.fori_loop(0, n - 1, one, 0)
-        own_back(slot).start()
 
     def own_back(slot):
         return pltpu.make_async_copy(
@@ -151,8 +181,14 @@
         return pltpu.make_async_copy(ref, ref, sem)
 
     many = (n - 1) * lats
-    for slot in range(slots):
-        send_out(slot)
+    early = first * GROUP
+    send_out(0, 0, early)
+    lax.fori_loop(first, groups, scatter_group, 0)
+    send_out(0, early, lats - early)
+    for slot in range(1, slots):
+        send_out(slot, 0, lats)
+    for slot in range(slots):
+        own_out(slot).start()
 
     for group in range(north // lanes):
         row = weight_ref[group : group + 1, :]
@@ -160,7 +196,6 @@
             jnp.broadcast_to(row, (lanes, lanes))
         )
 
-    lane = lax.broadcasted_iota(jnp.int32, (1, lanes), 1)
     lengths = degrees - (lane * degrees) // waves
     span = 2 * lanes
     part = lanes
@@ -180,7 +215,7 @@
             return carry
 
         lax.fori_loop(0, north // span, fold, 0)
-        mine = (own_ref[...] == me * slots + slot) & (lane < waves)
+        mine = (own_row[...] == me * slots + slot) & (lane < waves)
         length = jnp.sum(jnp.where(mine, lengths, 0), axis=1, keepdims=True)
 
         def direct(index, carry, slot=slot, length=length):
@@ -216,13 +251,20 @@
             return carry
 
         lax.fori_loop(0, north // span, inverse, 0)
-        send_back(slot)
+        if slot < slots - 1:
+            send_back(slot, 0, lats, slot)
+        else:
+            send_back(slot, 0, early, slot)
+            send_back(slot, early, lats - early, slots)
+        own_back(slot).start()
 
     pair_rows = 2 * levels
     row = lax.broadcasted_iota(jnp.int32, (pair_rows, lanes), 0)
     column = lax.broadcasted_iota(jnp.int32, (pair_rows, lanes), 1)
     level, level2 = row % levels, (column % lf) // fields
-    depth = depth_ref[...]
+    depth = jnp.zeros((pair_rows, lanes), jnp.float32)
+    for index in range(levels):
+        depth = jnp.where(level2 == index, depth_ref[index], depth)
     term = jnp.where(level2 > level, depth, jnp.where(level2 == level, 0.5 * depth, 0.0))
     fits = (row // levels == column // lf) & (column % fields == 0)
     term = jnp.where(fits, term, 0.0)
@@ -232,7 +274,8 @@
 
     for slot in range(slots):
         own_back(slot).wait()
-        all_of(returned.at[pl.ds(0, n - 1)], recv_sem.at[1, slot]).wait()
+        count = lats if slot < slots - 1 else early
+        all_of(returned.at[pl.ds(0, n - 1), pl.ds(0, count)], recv_sem.at[1, slot]).wait()
 
     def gather_group(group, carry):
         start = pl.multiple_of(group * GROUP, GROUP)
@@ -253,9 +296,16 @@
                 lat = lat_of(turn + h)
                 out_ref[lat] = two[h * lf : (h + 1) * lf]
                 geo_ref[lat] = heights[h * levels : (h + 1) * levels]
+        for copy in out_copies(group):
+            copy.start()
         return carry
 
-    lax.fori_loop(0, lats // GROUP, gather_group, 0)
+    lax.fori_loop(0, first, gather_group, 0)
+    all_of(returned.at[pl.ds(0, n - 1), pl.ds(early, lats - early)], recv_sem.at[1, slots]).wait()
+    lax.fori_loop(first, groups, gather_group, 0)
+    for group in range(groups):
+        for copy in out_copies(group):
+            copy.wait()
 
     for slot in range(slots):
         all_of(outgoing.at[pl.ds(0, n - 1)], send_sem.at[0, slot]).wait()
@@ -279,8 +329,8 @@
     waves = n * slots
     whole = n * lats
     assert lanes == 2 * waves and lanes == 2 * lf and whole == 2 * north
-    own = jnp.concatenate([owner, owner + waves]).reshape(1, lanes)
-    depth = jnp.tile(jnp.repeat(layer_depth, fields), 2).reshape(1, lanes)
+    far = pl.BlockSpec(memory_space=pltpu.HBM)
+    smem = pl.BlockSpec(memory_space=pltpu.SMEM)
     vmem = pl.BlockSpec(memory_space=pltpu.VMEM)
     fields_out, geopotential = pl.pallas_call(
         functools.partial(kernel, n, slots, 2 * half),
@@ -288,9 +338,13 @@
             jax.ShapeDtypeStruct((lats, lf, lanes), jnp.bfloat16),
             jax.ShapeDtypeStruct((lats, levels, lanes), jnp.bfloat16),
         ),
-        in_specs=[vmem] * 4 + [pl.BlockSpec(memory_space=pl.ANY)],
-        out_specs=(vmem, vmem),
+        in_specs=[far, smem, smem, vmem, far],
+        out_specs=(far, far),
         scratch_shapes=[
+            pltpu.VMEM((lats, lf, lanes), jnp.bfloat16),
+            pltpu.VMEM((lats, lf, lanes), jnp.bfloat16),
+            pltpu.VMEM((lats, levels, lanes), jnp.bfloat16),
+            pltpu.VMEM((1, lanes), jnp.int32),
             pltpu.VMEM(legendre.shape, jnp.bfloat16),
             pltpu.VMEM((waves, lats, lanes), jnp.bfloat16),
             pltpu.VMEM((slots * whole, lanes), jnp.bfloat16),
@@ -299,13 +353,15 @@
             pltpu.VMEM((2, half, lanes), jnp.bfloat16),
             pltpu.VMEM((slots * whole, lanes), jnp.bfloat16),
             pltpu.VMEM((waves, lats, lanes), jnp.bfloat16),
+            pltpu.SemaphoreType.DMA((lats // GROUP,)),
+            pltpu.SemaphoreType.DMA((2, lats // GROUP)),
             pltpu.SemaphoreType.DMA((slots,)),
             pltpu.SemaphoreType.DMA((2, slots)),
-            pltpu.SemaphoreType.DMA((2, slots)),
+            pltpu.SemaphoreType.DMA((2, slots + 1)),
             pltpu.SemaphoreType.DMA((2, slots)),
         ],
         compiler_params=pltpu.CompilerParams(
-            collective_id=0, has_side_effects=True, vmem_limit_bytes=48 * 2**20
+            collective_id=0, has_side_effects=True, vmem_limit_bytes=60 * 2**20
         ),
         cost_estimate=pl.CostEstimate(
             flops=16 * slots * half * north * lanes,
@@ -314,8 +370,8 @@
         ),
     )(
         fourier.reshape(lats, lf, lanes),
-        own,
-        depth,
+        owner,
+        layer_depth,
         quad_weights.reshape(north // lanes, lanes),
         legendre,
     )

time: 74.6 us -> 72.4 us (0.971)
  other arithmetic: 1.39 us -> 0 us
  local copies, waits for them, and re-layouts: 4.69 us -> 3.75 us
    unnamed x6 -> x4, local copies, waits for them, and re-layouts: 3.8 us -> 3.75 us
where the time goes in v2:
time: 72.4 us; the launch traced here: 72.2 us
  Pallas kernels  67.8 us (94%)
  local copies, waits for them, and re-layouts  3.75 us (5%)
    pallas_call x1, Pallas kernels, on_device(): pl.pallas_call(functools.partial(kernel, n, slots, 2 * half), out_shape=(...  67.8 us
    unnamed x4, local copies, waits for them, and re-layouts  3.75 us

profile of v2, /device:TPU:0, one launch (start us, length us, event | category | flops | bytes accessed | tf_op | source)
XLA Modules:
  0.0 72.2 jit_solution(16117511600663171184)
XLA Ops:
  0.6 67.8 %shard_map.68 = (bf16[80,64,128]{2,1,0:T(8,128)(2,1)}, bf16[80,16,128]{2,1,0:T(8,128)(2,1)}) custom-call(bf16[80,64,128]{2,1,0:T(8,128)(2,1)} %bitcast.4, s32[64]{0:T(128)} %own_ref.1, f32[16]{0:T(128)} %depth_ref.1, f32[10,128]{1,0:T(8,128)} %bitcast.5, bf16[2,2,640,1280]{3,2,1,0:T(8,128)(2,1)} %table_hbm.1), custom_call_target="tpu_custom_call" | custom-call | flops 3355443200 | bytes 9175040 | tf_op jit(solution)/shard_map/pallas_call | solution.py:335
  68.4 0.0 copy-start
  68.4 3.0 %copy.9 = bf16[80,16,4,128]{3,2,1,0:T(4,128)(2,1)} copy(bf16[80,16,4,128]{3,2,1,0:T(4,128)(2,1)} %bitcast.3) | data formatting | bytes 2621440
  71.5 0.0 copy-done
  71.5 0.7 %copy.10 = bf16[80,16,128]{2,1,0:T(8,128)(2,1)} copy(bf16[80,16,128]{2,1,0:T(8,128)(2,1)S(1)} %copy-done) | data formatting | bytes 655360
Async XLA Ops:
  68.4 3.0 %copy-start = (bf16[80,16,128]{2,1,0:T(8,128)(2,1)S(1)}, bf16[80,16,128]{2,1,0:T(8,128)(2,1)}, u32[]{:S(2)}) copy-start(bf16[80,16,128]{2,1,0:T(8,128)(2,1)} %get-tuple-element.9) | copy-start | bytes 983044

commit v3 on v2

--- a/solution.py
+++ b/solution.py
@@ -29,6 +29,7 @@
     geo_ref,
     own_row,
     tables,
+    turned,
     outgoing,
     arrived,
     weights,
@@ -202,6 +203,18 @@
 
     for slot in range(slots):
         table_copy(slot).wait()
+
+        def turn_over(index, carry, slot=slot):
+            start = pl.multiple_of(index * part, part)
+            for parity in range(2):
+                turned[slot, parity, pl.ds(start, part), :] = jnp.transpose(
+                    tables[slot, parity, :, pl.ds(start, part)]
+                )
+            return carry
+
+        lax.fori_loop(0, north // part, turn_over, 0)
+
+    for slot in range(slots):
         own_out(slot).wait()
         all_of(rows(arrived, slot * whole, many), recv_sem.at[0, slot]).wait()
 
@@ -236,10 +249,9 @@
         def inverse(index, carry, slot=slot):
             start = pl.multiple_of(index * span, span)
             even, odd = (
-                lax.dot_general(
-                    tables[slot, parity, :, pl.ds(start, span)],
+                jnp.dot(
+                    turned[slot, parity, pl.ds(start, span), :],
                     spectra[parity],
-                    TN,
                     preferred_element_type=jnp.float32,
                 )
                 for parity in range(2)
@@ -346,6 +358,7 @@
             pltpu.VMEM((lats, levels, lanes), jnp.bfloat16),
             pltpu.VMEM((1, lanes), jnp.int32),
             pltpu.VMEM(legendre.shape, jnp.bfloat16),
+            pltpu.VMEM((slots, 2, north, half), jnp.bfloat16),
             pltpu.VMEM((waves, lats, lanes), jnp.bfloat16),
             pltpu.VMEM((slots * whole, lanes), jnp.bfloat16),
             pltpu.VMEM((north, lanes), jnp.float32),
@@ -361,7 +374,7 @@
             pltpu.SemaphoreType.DMA((2, slots)),
         ],
         compiler_params=pltpu.CompilerParams(
-            collective_id=0, has_side_effects=True, vmem_limit_bytes=60 * 2**20
+            collective_id=0, has_side_effects=True, vmem_limit_bytes=52 * 2**20
         ),
         cost_estimate=pl.CostEstimate(
             flops=16 * slots * half * north * lanes,

time: 72.4 us -> 71.9 us (level)
    unnamed x4 -> x8, local copies, waits for them, and re-layouts: 3.75 us -> 3.78 us
where the time goes in v3:
time: 71.9 us; the launch traced here: 71.6 us
  Pallas kernels  67.2 us (93%)
  local copies, waits for them, and re-layouts  3.78 us (5%)
    pallas_call x1, Pallas kernels, on_device(): pl.pallas_call(functools.partial(kernel, n, slots, 2 * half), out_shape=(...  67.2 us
    unnamed x8, local copies, waits for them, and re-layouts  3.78 us

profile of v3, /device:TPU:0, one launch (start us, length us, event | category | flops | bytes accessed | tf_op | source)
XLA Modules:
  0.0 71.6 jit_solution(6579840173995125680)
XLA Ops:
  0.6 0.0 copy-start
  0.6 0.7 copy-done
  1.3 0.0 copy-start.1
  1.3 0.7 copy-done.1
  2.0 0.0 copy-start.2
  2.0 0.7 copy-done.2
  2.6 67.2 %shard_map.68 = (bf16[80,64,128]{2,1,0:T(8,128)(2,1)S(1)}, bf16[80,16,128]{2,1,0:T(8,128)(2,1)S(1)}) custom-call(bf16[80,64,128]{2,1,0:T(8,128)(2,1)} %bitcast.5, s32[64]{0:T(128)S(1)} %copy-done.1, f32[16]{0:T(128)S(1)} %copy-done.2, f32[10,128]{1,0:T(8,128)S(1)} %bitcast.4, bf16[2,2,640,1280]{3,2,1,0:T(8,128)(2,1)} %table_hbm.1), custom_call_target="tpu_custom_call" | custom-call | flops 3355443200 | bytes 9175040 | tf_op jit(solution)/shard_map/pallas_call | solution.py:347
  69.8 1.1 %copy.9 = bf16[80,16,4,128]{3,2,1,0:T(4,128)(2,1)} copy(bf16[80,16,4,128]{3,2,1,0:T(4,128)(2,1)S(1)} %bitcast.3) | data formatting | bytes 2621440
  70.9 0.7 %copy.10 = bf16[80,16,128]{2,1,0:T(8,128)(2,1)} copy(bf16[80,16,128]{2,1,0:T(8,128)(2,1)S(1)} %get-tuple-element.9) | data formatting | bytes 655360
Async XLA Ops:
  0.6 0.7 copy-start
  1.3 0.7 copy-start.1
  2.0 0.7 copy-start.2

commit v4 on v3

--- a/solution.py
+++ b/solution.py
@@ -18,8 +18,6 @@
     slots,
     degrees,
     x_hbm,
-    own_ref,
-    depth_ref,
     weight_ref,
     table_hbm,
     out_hbm,
@@ -95,9 +93,9 @@
 
     rows_i = lax.broadcasted_iota(jnp.int32, (lanes, lanes), 0)
     lane = lax.broadcasted_iota(jnp.int32, (1, lanes), 1)
-    owner = jnp.zeros((1, lanes), jnp.int32)
-    for wave in range(waves):
-        owner = jnp.where(lane % waves == wave, own_ref[wave], owner)
+    last_row = tables.shape[3] // lanes
+    small = weight_ref[last_row : last_row + 1, :]
+    owner = jnp.where(lane < waves, small, pltpu.roll(small, waves, 1)).astype(jnp.int32)
     own_row[...] = owner + waves * (lane // waves)
     permute = jnp.where(rows_i == own_row[...], 1.0, 0.0).astype(jnp.bfloat16)
     low = lax.broadcasted_iota(jnp.int32, (waves, lanes), 1) < lf
@@ -276,7 +274,8 @@
     level, level2 = row % levels, (column % lf) // fields
     depth = jnp.zeros((pair_rows, lanes), jnp.float32)
     for index in range(levels):
-        depth = jnp.where(level2 == index, depth_ref[index], depth)
+        value = jnp.sum(jnp.where(lane == waves + index, small, 0.0), axis=1, keepdims=True)
+        depth = jnp.where(level2 == index, value, depth)
     term = jnp.where(level2 > level, depth, jnp.where(level2 == level, 0.5 * depth, 0.0))
     fits = (row // levels == column // lf) & (column % fields == 0)
     term = jnp.where(fits, term, 0.0)
@@ -340,9 +339,17 @@
     slots, _, half, north = legendre.shape
     waves = n * slots
     whole = n * lats
-    assert lanes == 2 * waves and lanes == 2 * lf and whole == 2 * north
+    assert lanes == 2 * waves and lanes == 2 * lf and whole == 2 * north and levels <= waves
     far = pl.BlockSpec(memory_space=pltpu.HBM)
-    smem = pl.BlockSpec(memory_space=pltpu.SMEM)
+    packed_rows = north // lanes + 1
+    packed_size = packed_rows * lanes
+
+    def laid(values, start):
+        after = packed_size - start - values.shape[0]
+        zero = jnp.zeros((), values.dtype)
+        return lax.pad(values, zero, [(start, after, 0)]).astype(jnp.float32)
+
+    packed = laid(quad_weights, 0) + laid(owner, north) + laid(layer_depth, north + waves)
     vmem = pl.BlockSpec(memory_space=pltpu.VMEM)
     fields_out, geopotential = pl.pallas_call(
         functools.partial(kernel, n, slots, 2 * half),
@@ -350,7 +357,7 @@
             jax.ShapeDtypeStruct((lats, lf, lanes), jnp.bfloat16),
             jax.ShapeDtypeStruct((lats, levels, lanes), jnp.bfloat16),
         ),
-        in_specs=[far, smem, smem, vmem, far],
+        in_specs=[far, vmem, far],
         out_specs=(far, far),
         scratch_shapes=[
             pltpu.VMEM((lats, lf, lanes), jnp.bfloat16),
@@ -383,9 +390,7 @@
         ),
     )(
         fourier.reshape(lats, lf, lanes),
-        owner,
-        layer_depth,
-        quad_weights.reshape(north // lanes, lanes),
+        packed.reshape(packed_rows, lanes),
         legendre,
     )
     fields_out = fields_out.reshape(lats, levels, fields, lanes)

time: 71.9 us -> 71 us (0.987)
  local copies, waits for them, and re-layouts: 3.78 us -> 1.78 us
  other arithmetic: 0 us -> 0.8 us
    unnamed x8 -> x2, local copies, waits for them, and re-layouts: 3.78 us -> 1.78 us
    reshape x0 -> x1, other arithmetic: none -> 0.8 us  [on_device(): packed.reshape(packed_rows, lanes)]
where the time goes in v4:
time: 71 us; the launch traced here: 70.8 us
  Pallas kernels  67.5 us (95%)
  local copies, waits for them, and re-layouts  1.78 us (3%)
  other arithmetic  0.8 us (1%)
    pallas_call x1, Pallas kernels, on_device(): pl.pallas_call(functools.partial(kernel, n, slots, 2 * half), out_shape=(...  67.5 us
    unnamed x2, local copies, waits for them, and re-layouts  1.78 us

profile of v4, /device:TPU:0, one launch (start us, length us, event | category | flops | bytes accessed | tf_op | source)
XLA Modules:
  0.0 70.8 jit_solution(16726526017255190013)
XLA Ops:
  0.6 0.8 %add_bitcast_fusion.weight_ref = f32[11,128]{1,0:T(8,128)S(1)} fusion(f32[16]{0:T(128)} %param.9, s32[64]{0:T(128)} %param.6, f32[1280]{0:T(1024)} %param.8), kind=kLoop, calls=%fused_computation | loop fusion | flops 4224 | bytes 11072 | tf_op jit(solution)/shard_map/reshape | solution.py:393
  1.4 67.5 %shard_map.68 = (bf16[80,64,128]{2,1,0:T(8,128)(2,1)S(1)}, bf16[80,16,128]{2,1,0:T(8,128)(2,1)S(1)}) custom-call(bf16[80,64,128]{2,1,0:T(8,128)(2,1)} %bitcast.5, f32[11,128]{1,0:T(8,128)S(1)} %add_bitcast_fusion.weight_ref, bf16[2,2,640,1280]{3,2,1,0:T(8,128)(2,1)} %table_hbm.1), custom_call_target="tpu_custom_call" | custom-call | flops 3355443200 | bytes 9175040 | tf_op jit(solution)/shard_map/pallas_call | solution.py:354
  69.0 1.1 %copy.9 = bf16[80,16,4,128]{3,2,1,0:T(4,128)(2,1)} copy(bf16[80,16,4,128]{3,2,1,0:T(4,128)(2,1)S(1)} %bitcast.4) | data formatting | bytes 2621440
  70.0 0.7 %copy.10 = bf16[80,16,128]{2,1,0:T(8,128)(2,1)} copy(bf16[80,16,128]{2,1,0:T(8,128)(2,1)S(1)} %get-tuple-element.9) | data formatting | bytes 655360
